TPU v7x, 32 devices: a whole 2x2x4 slice. The times are simulated.
32 devices in a mesh: layer: 2 (over x), row: 4 (over z), col: 4 (over y, core).
Axes of the slice: x: 2, y: 2, z: 4, core: 2. Of those that a mesh axis runs over, the one named last changes fastest.
Arguments:
- rhs_root: float32 [16384, 128], P('col'), may hold values from -6 to 6
- rhs_child: float32 [2, 8192, 128], P('layer', 'col'), may hold values from -6 to 6
- rhs_leaf: float32 [4, 4096, 128], P('layer', 'col'), may hold values from -6 to 6
- root_inv: bfloat16 [16384, 16384], P('row', 'col'), may hold values from -0.046875 to 0.046875
- child_inv: bfloat16 [2, 8192, 8192], P('layer', 'row', 'col'), may hold values from -0.0625 to 0.0625
- leaf_inv: bfloat16 [4, 4096, 4096], P('layer', 'row', 'col'), may hold values from -0.09375 to 0.09375
- leaf_to_child: bfloat16 [4, 8192, 4096], P('layer', 'col', 'row'), may hold values from -0.0625 to 0.0625
- leaf_to_root: bfloat16 [4, 16384, 4096], P('layer', 'col', 'row'), may hold values from -0.03125 to 0.03125
- child_to_root: bfloat16 [2, 16384, 8192], P('layer', 'col', 'row'), may hold values from -0.03125 to 0.03125
Outputs:
- x_root: float32 [16384, 128], P('col')
- x_child: float32 [2, 8192, 128], P('layer', 'col')
- x_leaf: float32 [4, 4096, 128], P('layer', 'col')
- y_root: float32 [16384, 128], P('row')
All inputs are finite; a program needn't handle non-finite values.
Results may differ from a plain program's by a relative error of at most 0.008.
Values sent between devices are 32-bit elements; how exact they have to be, the bound alone decides.
A program may use at most 192 MiB of HBM per device.

v0:
```python
import jax
import jax.numpy as jnp
from jax import lax
from jax.sharding import PartitionSpec as P


def col_sum(values):
    return lax.psum(values, "col")


def row_sum(values):
    return lax.psum(values, "row")


def root_total(values):
    return lax.psum(values, ("layer", "row"))


def half16(values):
    return values.astype(jnp.bfloat16)


def on_device(
    rhs_root,
    rhs_child,
    rhs_leaf,
    root_inv,
    child_inv,
    leaf_inv,
    leaf_to_child,
    leaf_to_root,
    child_to_root,
):
    f32 = jnp.float32
    y_leaf = col_sum(
        jnp.einsum("gij,gjs->gis", leaf_inv, half16(rhs_leaf), preferred_element_type=f32)
    )
    leaf_bf = half16(y_leaf)
    leaf_update = jnp.einsum("gij,gjs->is", leaf_to_root, leaf_bf, preferred_element_type=f32)
    r_child = rhs_child[0] - row_sum(
        jnp.einsum("gij,gjs->is", leaf_to_child, leaf_bf, preferred_element_type=f32)
    )
    y_child = col_sum(jnp.dot(child_inv[0], half16(r_child), preferred_element_type=f32))
    child_update = jnp.dot(child_to_root[0], half16(y_child), preferred_element_type=f32)
    r_root = rhs_root - root_total(child_update + leaf_update)
    y_root = col_sum(jnp.dot(root_inv, half16(r_root), preferred_element_type=f32))
    x_root = row_sum(jnp.einsum("ij,is->js", root_inv, half16(y_root), preferred_element_type=f32))
    root_bf = half16(x_root)
    back_child = y_child - col_sum(
        jnp.einsum("ij,is->js", child_to_root[0], root_bf, preferred_element_type=f32)
    )
    x_child = row_sum(
        jnp.einsum("ij,is->js", child_inv[0], half16(back_child), preferred_element_type=f32)
    )
    terms = jnp.einsum("gij,is->gjs", leaf_to_child, half16(x_child), preferred_element_type=f32)
    terms = terms + jnp.einsum("gij,is->gjs", leaf_to_root, root_bf, preferred_element_type=f32)
    back_leaf = y_leaf - col_sum(terms)
    x_leaf = row_sum(
        jnp.einsum("gij,gis->gjs", leaf_inv, half16(back_leaf), preferred_element_type=f32)
    )
    return (x_root, x_child[None], x_leaf, y_root)


def solution(mesh):
    in_specs = (
        P("col", None),
        P("layer", "col", None),
        P("layer", "col", None),
        P("row", "col"),
        P("layer", "row", "col"),
        P("layer", "row", "col"),
        P("layer", "col", "row"),
        P("layer", "col", "row"),
        P("layer", "col", "row"),
    )
    out_specs = (P("col", None), P("layer", "col", None), P("layer", "col", None), P("row", None))
    return jax.shard_map(
        on_device, mesh=mesh, in_specs=in_specs, out_specs=out_specs, check_vma=False
    )
```

profile of v0, /device:TPU:0, one launch (start us, length us, event | category | flops | bytes accessed | tf_op | source)
XLA Modules:
  0.0 654.0 jit_solution(8513085060972129987)
XLA Ops:
  7.2 4.7 fusion.34
  11.9 0.0 all-reduce.13.cloned.1.call-start
  12.0 38.9 %all-reduce.11.cloned.1.call-done = f32[2,1024,128]{2,1,0:T(8,128)} async-done(((f32[2,1024,128]{2,1,0:T(8,128)}), f32[2,1024,128]{2,1,0:T(8,128)}) %all-reduce.11.cloned.1.call-update) | async-done | bytes 1048592 | tf_op jit(solution)/shard_map/psum | solution.py:8
  50.9 6.9 %convolution_bitcast_fusion.3 = f32[2048,128]{1,0:T(8,128)} fusion(bf16[2,2048,1024]{2,1,0:T(8,128)(2,1)} %param.15, f32[2,1024,128]{2,1,0:T(8,128)} %all-reduce.11.cloned.1.call-done), kind=kOutput, calls=%fused_computation.15 | convolution fusion | flops 1074003968 | bytes 10485760 | tf_op jit(solution)/shard_map/gij,gjs->is/dot_general | solution.py:41
  57.9 0.0 all-reduce.15.cloned.1.call-start
  57.9 52.3 %all-reduce.13.cloned.1.call-done = f32[2048,128]{1,0:T(8,128)} async-done(((f32[2048,128]{1,0:T(8,128)}), f32[2048,128]{1,0:T(8,128)}) %all-reduce.13.cloned.1.call-update) | async-done | bytes 1048592 | tf_op jit(solution)/shard_map/psum | solution.py:12
  110.2 7.6 %fusion.14 = f32[2048,128]{0,1:T(8,128)} fusion(bf16[1,2048,2048]{2,1,0:T(8,128)(2,1)} %param.13, f32[2048,128]{1,0:T(8,128)} %all-reduce.13.cloned.1.call-done, f32[1,2048,128]{2,1,0:T(8,128)S(1)} %copy-done.3), kind=kOutput, calls=%fused_computation.13 | convolution fusion | flops 1074266112 | bytes 11534336 | tf_op jit(solution)/shard_map/dot_general | solution.py:43
  117.9 0.2 all-reduce.17.cloned.1.call-start
  118.1 10.5 %convolution_bitcast_fusion = f32[128,4096]{0,1:T(8,128)S(1)} fusion(bf16[2,4096,1024]{2,1,0:T(8,128)(2,1)} %param.16, f32[2,1024,128]{2,1,0:T(8,128)S(1)} %copy-done.1), kind=kOutput, calls=%fused_computation.8 | convolution fusion | flops 2147745792 | bytes 19922944 | tf_op jit(solution)/shard_map/gij,gjs->is/dot_general | solution.py:39
  128.6 24.9 %all-reduce.15.cloned.1.call-done = f32[2048,128]{0,1:T(8,128)} async-done(((f32[2048,128]{0,1:T(8,128)}), f32[2048,128]{0,1:T(8,128)}) %all-reduce.15.cloned.1.call-update) | async-done | bytes 1048592 | tf_op jit(solution)/shard_map/psum | solution.py:8
  153.5 12.0 %fusion.11 = f32[4096,128]{1,0:T(8,128)} fusion(f32[128,4096]{0,1:T(8,128)S(1)} %convolution_bitcast_fusion, bf16[1,4096,2048]{2,1,0:T(8,128)(2,1)} %param.17, f32[2048,128]{0,1:T(8,128)} %all-reduce.15.cloned.1.call-done), kind=kOutput, calls=%fused_computation.12 | convolution fusion | flops 2148270080 | bytes 22020096 | tf_op jit(solution)/shard_map/dot_general | solution.py:44
  165.5 0.3 all-reduce.19.cloned.1.call-start
  165.7 102.1 %all-reduce.17.cloned.1.call-done = f32[4096,128]{1,0:T(8,128)} async-done(((f32[4096,128]{1,0:T(8,128)}), f32[4096,128]{1,0:T(8,128)}) %all-reduce.17.cloned.1.call-update) | async-done | bytes 2097168 | tf_op jit(solution)/shard_map/psum | solution.py:16
  267.8 18.2 %convolution_bitcast_fusion.2 = f32[4096,128]{0,1:T(8,128)} fusion(bf16[4096,4096]{1,0:T(8,128)(2,1)} %param.12, f32[4096,128]{1,0:T(8,128)} %param.9, f32[4096,128]{1,0:T(8,128)} %all-reduce.17.cloned.1.call-done), kind=kOutput, calls=%fused_computation.10 | convolution fusion | flops 4296015872 | bytes 39845888 | tf_op jit(solution)/shard_map/dot_general | solution.py:46
  286.1 51.2 %all-reduce.19.cloned.1.call-done = f32[4096,128]{0,1:T(8,128)} async-done(((f32[4096,128]{0,1:T(8,128)}), f32[4096,128]{0,1:T(8,128)}) %all-reduce.19.cloned.1.call-update) | async-done | bytes 2097168 | tf_op jit(solution)/shard_map/psum | solution.py:8
  337.4 17.0 %convolution_bitcast_fusion.1 = f32[4096,128]{0,1:T(8,128)} fusion(bf16[4096,4096]{1,0:T(8,128)(2,1)} %param.12, f32[4096,128]{0,1:T(8,128)} %all-reduce.19.cloned.1.call-done), kind=kOutput, calls=%fused_computation.9 | convolution fusion | flops 4295491584 | bytes 37748736 | tf_op jit(solution)/shard_map/ij,is->js/dot_general | solution.py:47
  354.4 86.7 %all-reduce.21.cloned.1.call-done = f32[4096,128]{0,1:T(8,128)} async-done(((f32[4096,128]{0,1:T(8,128)}), f32[4096,128]{0,1:T(8,128)}) %all-reduce.21.cloned.1.call-update) | async-done | bytes 2097168 | tf_op jit(solution)/shard_map/psum | solution.py:12
  441.1 9.7 %fusion.20 = f32[2048,128]{0,1:T(8,128)} fusion(bf16[1,4096,2048]{2,1,0:T(8,128)(2,1)} %param.17, f32[4096,128]{0,1:T(8,128)} %all-reduce.21.cloned.1.call-done), kind=kOutput, calls=%fused_computation.16 | convolution fusion | flops 2148007936 | bytes 19922944 | tf_op jit(solution)/shard_map/ij,is->js/dot_general | solution.py:50
  450.9 0.0 all-reduce.25.cloned.1.call-start
  450.9 35.2 %all-reduce.23.cloned.1.call-done = f32[2048,128]{0,1:T(8,128)} async-done(((f32[2048,128]{0,1:T(8,128)}), f32[2048,128]{0,1:T(8,128)}) %all-reduce.23.cloned.1.call-update) | async-done | bytes 1048592 | tf_op jit(solution)/shard_map/psum | solution.py:8
  486.1 6.3 fusion.17
  492.4 0.3 all-reduce.27.cloned.1.call-start
  492.7 11.1 %fusion.24 = f32[128,2,1024]{0,2,1:T(8,128)} fusion(bf16[2,4096,1024]{2,1,0:T(8,128)(2,1)} %param.16, f32[4096,128]{0,1:T(8,128)S(1)} %copy-done), kind=kOutput, calls=%fused_computation.21 | convolution fusion | flops 2148007936 | bytes 19922944 | tf_op jit(solution)/shard_map/gij,is->gjs/dot_general | solution.py:56
  503.8 40.9 %all-reduce.25.cloned.1.call-done = f32[2048,128]{0,1:T(8,128)} async-done(((f32[2048,128]{0,1:T(8,128)}), f32[2048,128]{0,1:T(8,128)}) %all-reduce.25.cloned.1.call-update) | async-done | bytes 1048592 | tf_op jit(solution)/shard_map/psum | solution.py:12
  544.7 7.7 %fusion.23 = f32[2,1024,128]{2,1,0:T(8,128)} fusion(f32[128,2,1024]{0,2,1:T(8,128)} %fusion.24, bf16[2,2048,1024]{2,1,0:T(8,128)(2,1)} %param.15, f32[2048,128]{0,1:T(8,128)} %all-reduce.25.cloned.1.call-done), kind=kOutput, calls=%fused_computation.20 | convolution fusion | flops 1074266112 | bytes 11534336 | tf_op jit(solution)/shard_map/gij,is->gjs/dot_general | solution.py:55
  552.4 35.5 %all-reduce.27.cloned.1.call-done = f32[2,1024,128]{2,1,0:T(8,128)} async-done(((f32[2,1024,128]{2,1,0:T(8,128)}), f32[2,1024,128]{2,1,0:T(8,128)}) %all-reduce.27.cloned.1.call-update) | async-done | bytes 1048592 | tf_op jit(solution)/shard_map/psum | solution.py:8
  588.0 4.3 convolution_bitcast_fusion.4
  592.3 3.0 copy.17
  595.2 1.8 copy.14
  597.0 1.3 copy.15
  598.3 46.3 %all-reduce.29.cloned.1.call-done = f32[2,1024,128]{1,2,0:T(8,128)} async-done(((f32[2,1024,128]{1,2,0:T(8,128)}), f32[2,1024,128]{1,2,0:T(8,128)}) %all-reduce.29.cloned.1.call-update) | async-done | bytes 1048592 | tf_op jit(solution)/shard_map/psum | solution.py:12
  644.6 2.5 copy.16
  (22 shorter events, 0.3 us)
Async XLA Ops:
  7.2 43.8 %all-reduce.11.cloned.1.call-start = ((), (), s32[]{:S(2)}) async-start(), calls=%async_computation | async-start | bytes 2097152 | tf_op jit(solution)/shard_map/psum | solution.py:8
  11.9 98.3 %copy-start.3 = (f32[1,2048,128]{2,1,0:T(8,128)S(1)}, f32[1,2048,128]{2,1,0:T(8,128)}, u32[]{:S(2)}) copy-start(f32[1,2048,128]{2,1,0:T(8,128)} %param.10) | copy-start | bytes 3145732
  11.9 98.3 %all-reduce.13.cloned.1.call-start = ((), (), s32[]{:S(2)}) async-start(), calls=%async_computation.1 | async-start | bytes 2097152 | tf_op jit(solution)/shard_map/psum | solution.py:12
  57.9 60.2 %copy-start.1 = (f32[2,1024,128]{2,1,0:T(8,128)S(1)}, f32[2,1024,128]{2,1,0:T(8,128)}, u32[]{:S(2)}) copy-start(f32[2,1024,128]{2,1,0:T(8,128)} %all-reduce.11.cloned.1.call-done) | copy-start | bytes 3145732
  57.9 95.6 %all-reduce.15.cloned.1.call-start = ((), (), s32[]{:S(2)}) async-start(), calls=%async_computation.2 | async-start | bytes 2097152 | tf_op jit(solution)/shard_map/psum | solution.py:8
  117.9 150.0 %all-reduce.17.cloned.1.call-start = ((), (), s32[]{:S(2)}) async-start(), calls=%async_computation.3 | async-start | bytes 4194304 | tf_op jit(solution)/shard_map/psum | solution.py:16
  165.5 171.9 %all-reduce.19.cloned.1.call-start = ((), (), s32[]{:S(2)}) async-start(), calls=%async_computation.4 | async-start | bytes 4194304 | tf_op jit(solution)/shard_map/psum | solution.py:8
  286.1 155.0 %all-reduce.21.cloned.1.call-start = ((), (), s32[]{:S(2)}) async-start(), calls=%async_computation.5 | async-start | bytes 4194304 | tf_op jit(solution)/shard_map/psum | solution.py:12
  354.4 131.7 %all-reduce.23.cloned.1.call-start = ((), (), s32[]{:S(2)}) async-start(), calls=%async_computation.6 | async-start | bytes 2097152 | tf_op jit(solution)/shard_map/psum | solution.py:8
  450.9 41.8 %copy-start = (f32[4096,128]{0,1:T(8,128)S(1)}, f32[4096,128]{0,1:T(8,128)}, u32[]{:S(2)}) copy-start(f32[4096,128]{0,1:T(8,128)} %all-reduce.21.cloned.1.call-done) | copy-start | bytes 6291460
  450.9 93.8 %all-reduce.25.cloned.1.call-start = ((), (), s32[]{:S(2)}) async-start(), calls=%async_computation.7 | async-start | bytes 2097152 | tf_op jit(solution)/shard_map/psum | solution.py:12
  492.4 95.6 %all-reduce.27.cloned.1.call-start = ((), (), s32[]{:S(2)}) async-start(), calls=%async_computation.8 | async-start | bytes 2097152 | tf_op jit(solution)/shard_map/psum | solution.py:8
  552.4 92.2 %all-reduce.29.cloned.1.call-start = ((), (), s32[]{:S(2)}) async-start(), calls=%async_computation.9 | async-start | bytes 2097152 | tf_op jit(solution)/shard_map/psum | solution.py:12
  592.2 4.8 copy-start.2
Sparse Core Ops, SparseCore 0:
  12.1 38.8 all-reduce.10
  58.0 52.1 all-reduce.12
  118.0 35.4 all-reduce.14
  165.6 102.2 all-reduce.16
  286.2 51.1 all-reduce.18
  354.5 86.5 all-reduce.20
  451.0 35.0 all-reduce.22
  492.5 52.1 all-reduce.24
  552.5 35.4 all-reduce.26
  592.4 52.1 all-reduce.28
where the time goes:
time: 654 us
  waiting for transfers between devices  514 us (79%)
  matrix products  116 us (18%)
  between operations  14.2 us (2%)
  local copies, waits for them, and re-layouts  8.62 us (1%)
    psum x4, waiting for transfers between devices, row_sum(): return lax.psum(values, 'row')  226 us
    psum x5, waiting for transfers between devices, col_sum(): return lax.psum(values, 'col')  186 us
    psum x1, waiting for transfers between devices, root_total(): return lax.psum(values, ('layer', 'row'))  102 us
    dot_general x1, matrix products, on_device(): jnp.dot(root_inv, half16(r_root), preferred_element_type=f32)  18.2 us
    dot_general x1, matrix products, on_device(): jnp.einsum('ij,is->js', root_inv, half16(y_root), preferred_element_type=...  17 us
  transfers between devices with their start and end apart: 10, of which 10 were waited for; matrix products, arithmetic and copies ran while one was open for 4% of the time, Pallas kernels for 0%

commit v1 on v0

v1 whole, which is shorter than its diff:
```python
import functools

import jax
import jax.numpy as jnp
from jax import lax
from jax.experimental import pallas as pl
from jax.experimental.pallas import tpu as pltpu
from jax.sharding import PartitionSpec as P

F32 = jnp.float32
CHUNKS = 8


def half16(values):
    return values.astype(jnp.bfloat16)


def remote(src, dst, send, recv, axis, index):
    return pltpu.make_async_remote_copy(
        src_ref=src,
        dst_ref=dst,
        send_sem=send,
        recv_sem=recv,
        device_id={axis: index},
        device_id_type=pl.DeviceIdType.MESH,
    )


def greet(partners):
    barrier = pltpu.get_barrier_semaphore()
    for axis, index in partners:
        pl.semaphore_signal(
            barrier, inc=1, device_id={axis: index}, device_id_type=pl.DeviceIdType.MESH
        )
    pl.semaphore_wait(barrier, len(partners))


def rows_at(start, size):
    return pl.ds(pl.multiple_of(start, 8), size)


def col_kernel(chunks, d, o, x, s, y, t, s0, r0, s1, r1, s2, r2):
    me = lax.axis_index("col")
    core, chip = lax.rem(me, 2), lax.div(me, 2)
    twin, across = 2 * chip + 1 - core, 2 * (1 - chip) + core
    half = d.shape[0] // 2
    size = half // chunks
    greet([("col", twin), ("col", across)])
    first, second, third = [], [], []
    for c in range(chunks):
        at = pl.ds(c * size, size)
        src = d.at[rows_at((1 - core) * half + c * size, size)]
        first.append(remote(src, x.at[at], s0.at[c], r0.at[c], "col", twin))
        first[-1].start()
    for c in range(chunks):
        at = pl.ds(c * size, size)
        first[c].wait_recv()
        s[at] = d[rows_at(core * half + c * size, size)] + x[at]
        second.append(remote(s.at[at], y.at[at], s1.at[c], r1.at[c], "col", across))
        second[-1].start()
    for c in range(chunks):
        at = pl.ds(c * size, size)
        mine = rows_at(core * half + c * size, size)
        second[c].wait_recv()
        t[mine] = s[at] + y[at]
        third.append(remote(t.at[mine], t.at[mine], s2.at[c], r2.at[c], "col", twin))
        third[-1].start()
    for c in range(chunks):
        third[c].wait_recv()
    o[...] = t[...]
    for copy in first + second + third:
        copy.wait_send()


def col_layer_kernel(chunks, d, o, x, u, w, s, y, t, s0, r0, s1, r1, s2, r2, s3, r3, s4, r4):
    me, layer = lax.axis_index("col"), lax.axis_index("layer")
    core, chip = lax.rem(me, 2), lax.div(me, 2)
    twin, across, other = 2 * chip + 1 - core, 2 * (1 - chip) + core, 1 - layer
    half = d.shape[0] // 2
    quarter = half // 2
    size = quarter // chunks
    greet([("col", twin), ("col", across), ("layer", other)])

    def place(core_of, layer_of, c):
        return rows_at(core_of * half + layer_of * quarter + c * size, size)

    cores, layers, chips, backs, gathers = [], [], [], [], []
    for g, part in enumerate((other, layer)):
        for c in range(chunks):
            i = g * chunks + c
            src = d.at[place(1 - core, part, c)]
            cores.append(
                remote(src, x.at[pl.ds(i * size, size)], s0.at[i], r0.at[i], "col", twin)
            )
            cores[-1].start()
    for c in range(chunks):
        at = pl.ds(c * size, size)
        cores[c].wait_recv()
        u[at] = d[place(core, other, c)] + x[at]
        layers.append(remote(u.at[at], w.at[at], s1.at[c], r1.at[c], "layer", other))
        layers[-1].start()
    for c in range(chunks):
        at = pl.ds(c * size, size)
        cores[chunks + c].wait_recv()
        layers[c].wait_recv()
        s[at] = d[place(core, layer, c)] + x[pl.ds((chunks + c) * size, size)] + w[at]
        chips.append(remote(s.at[at], y.at[at], s2.at[c], r2.at[c], "col", across))
        chips[-1].start()
    for c in range(chunks):
        at = pl.ds(c * size, size)
        mine = place(core, layer, c)
        chips[c].wait_recv()
        t[mine] = s[at] + y[at]
        backs.append(remote(t.at[mine], t.at[mine], s3.at[c], r3.at[c], "layer", other))
        backs[-1].start()
        gathers.append(remote(t.at[mine], t.at[mine], s4.at[c], r4.at[c], "col", twin))
        gathers[-1].start()
    for c in range(chunks):
        i = chunks + c
        theirs = place(core, other, c)
        backs[c].wait_recv()
        gathers.append(remote(t.at[theirs], t.at[theirs], s4.at[i], r4.at[i], "col", twin))
        gathers[-1].start()
    for copy in gathers:
        copy.wait_recv()
    o[...] = t[...]
    for copy in cores + layers + chips + backs + gathers:
        copy.wait_send()


def row_kernel(n, chunks, scatter, gather, d, o, acc, ab, w, t, s0, r0, s1, s2, rab, s3, r3):
    me, layer = lax.axis_index("row"), lax.axis_index("layer")
    other = 1 - layer
    left = me < n // 2
    middle = (me == n // 2 - 1) | (me == n // 2)
    inside = (me > 0) & (me < n - 1)
    inner = jnp.where(left, me + 1, me - 1)
    outer = jnp.where(left, jnp.maximum(me - 1, 0), jnp.minimum(me + 1, n - 1))
    slot = jnp.where(middle, 1, 0)
    rows = acc.shape[0]
    size = rows // chunks

    barrier = pltpu.get_barrier_semaphore()

    def signal(axis, index):
        pl.semaphore_signal(
            barrier, inc=1, device_id={axis: index}, device_id_type=pl.DeviceIdType.MESH
        )

    signal("row", inner)
    if scatter or gather:
        signal("layer", other)

    @pl.when(inside)
    def _():
        signal("row", outer)

    peers = 2 if scatter or gather else 1
    pl.semaphore_wait(barrier, peers + jnp.where(inside, 1, 0))

    def at(c):
        return pl.ds(c * size, size)

    def own(c):
        return rows_at(layer * rows + c * size, size) if gather else at(c)

    def swap(c):
        src = d.at[rows_at(other * rows + c * size, size)]
        return remote(src, w.at[at(c)], s0.at[c], r0.at[c], "layer", other)

    def inward(c):
        return remote(
            acc.at[at(c)], ab.at[slot, at(c)], s1.at[c], rab.at[slot, c], "row", inner
        )

    def from_outer(c):
        return remote(acc.at[at(c)], ab.at[0, at(c)], s1.at[c], rab.at[0, c], "row", inner)

    def outward(c):
        return remote(t.at[own(c)], ab.at[1, at(c)], s2.at[c], rab.at[1, c], "row", outer)

    def hand(c):
        return remote(t.at[own(c)], t.at[own(c)], s3.at[c], r3.at[c], "layer", other)

    def first(c, has_outer):
        if scatter:
            swap(c).wait_recv()
            mine = d[rows_at(layer * rows + c * size, size)] + w[at(c)]
        else:
            mine = d[at(c)]
        if has_outer:
            from_outer(c).wait_recv()
            mine = mine + ab[0, at(c)]
        acc[at(c)] = mine
        inward(c).start()

    def second(c, has_outer):
        outward(c).wait_recv()
        arrived = ab[1, at(c)]
        t[own(c)] = jnp.where(middle, acc[at(c)] + arrived, arrived)
        if has_outer:
            outward(c).start()
        if gather:
            hand(c).start()

    if scatter:
        for c in range(chunks):
            swap(c).start()

    @pl.when(inside)
    def _():
        for c in range(chunks + 1):
            if c < chunks:
                first(c, True)
            if c > 0:
                second(c - 1, True)
        for c in range(chunks):
            outward(c).wait_send()

    @pl.when(jnp.logical_not(inside))
    def _():
        for c in range(chunks):
            first(c, False)
        for c in range(chunks):
            second(c, False)

    for c in range(chunks):
        if gather:
            hand(c).wait_recv()
            hand(c).wait_send()
        if scatter:
            swap(c).wait_send()
        inward(c).wait_send()
    o[...] = t[...]


def run(kernel, rows, scratch, ident, values):
    return pl.pallas_call(
        kernel,
        out_shape=jax.ShapeDtypeStruct((rows, values.shape[1]), F32),
        in_specs=[pl.BlockSpec(memory_space=pltpu.VMEM)],
        out_specs=pl.BlockSpec(memory_space=pltpu.VMEM),
        scratch_shapes=scratch,
        compiler_params=pltpu.CompilerParams(
            collective_id=ident, has_side_effects=True, vmem_limit_bytes=24 * 2**20
        ),
    )(values)


def col_sum(values, ident):
    flat = values.reshape(-1, values.shape[-1])
    rows, wide = flat.shape
    sems = [pltpu.SemaphoreType.DMA((CHUNKS,))] * 6
    half = pltpu.VMEM((rows // 2, wide), F32)
    scratch = [half, half, half, pltpu.VMEM((rows, wide), F32)] + sems
    out = run(functools.partial(col_kernel, CHUNKS), rows, scratch, ident, flat)
    return out.reshape(values.shape)


def col_layer_sum(values, ident):
    rows, wide = values.shape
    one, two = pltpu.SemaphoreType.DMA((CHUNKS,)), pltpu.SemaphoreType.DMA((2 * CHUNKS,))
    quarter = pltpu.VMEM((rows // 4, wide), F32)
    scratch = [pltpu.VMEM((rows // 2, wide), F32)] + [quarter] * 4
    scratch += [pltpu.VMEM((rows, wide), F32), two, two] + [one] * 6 + [two, two]
    return run(functools.partial(col_layer_kernel, CHUNKS), rows, scratch, ident, values)


def row_sum(n, values, ident, scatter=False, gather=False):
    flat = values.reshape(-1, values.shape[-1])
    rows, wide = flat.shape
    if scatter:
        rows = rows // 2
    total = 2 * rows if gather else rows
    one = pltpu.SemaphoreType.DMA((CHUNKS,))
    scratch = [
        pltpu.VMEM((rows, wide), F32),
        pltpu.VMEM((2, rows, wide), F32),
        pltpu.VMEM((rows if scatter else 8, wide), F32),
        pltpu.VMEM((total, wide), F32),
        one,
        one,
        one,
        one,
        pltpu.SemaphoreType.DMA((2, CHUNKS)),
        one,
        one,
    ]
    kernel = functools.partial(row_kernel, n, CHUNKS, scatter, gather)
    out = run(kernel, total, scratch, ident, flat)
    return out if scatter or gather else out.reshape(values.shape)


def on_device(
    n,
    rhs_root,
    rhs_child,
    rhs_leaf,
    root_inv,
    child_inv,
    leaf_inv,
    leaf_to_child,
    leaf_to_root,
    child_to_root,
):
    layer = lax.axis_index("layer")
    wide = rhs_root.shape[0] // 2
    rhs_half = lax.dynamic_slice_in_dim(rhs_root, layer * wide, wide, 0)
    root_half = lax.dynamic_slice_in_dim(root_inv, layer * wide, wide, 1)

    y_leaf = col_sum(
        jnp.einsum("gij,gjs->gis", leaf_inv, half16(rhs_leaf), preferred_element_type=F32), 0
    )
    leaf_bf = half16(y_leaf)
    leaf_update = jnp.einsum("gij,gjs->is", leaf_to_root, leaf_bf, preferred_element_type=F32)
    r_child = rhs_child[0] - row_sum(
        n, jnp.einsum("gij,gjs->is", leaf_to_child, leaf_bf, preferred_element_type=F32), 1
    )
    y_child = col_sum(jnp.dot(child_inv[0], half16(r_child), preferred_element_type=F32), 2)
    child_update = jnp.dot(child_to_root[0], half16(y_child), preferred_element_type=F32)
    r_root = rhs_half - row_sum(n, child_update + leaf_update, 3, scatter=True)
    y_root = col_layer_sum(jnp.dot(root_half, half16(r_root), preferred_element_type=F32), 4)
    x_root = row_sum(
        n,
        jnp.einsum("ij,is->js", root_half, half16(y_root), preferred_element_type=F32),
        5,
        gather=True,
    )
    root_bf = half16(x_root)
    back_child = y_child - col_sum(
        jnp.einsum("ij,is->js", child_to_root[0], root_bf, preferred_element_type=F32), 6
    )
    x_child = row_sum(
        n,
        jnp.einsum("ij,is->js", child_inv[0], half16(back_child), preferred_element_type=F32),
        7,
    )
    terms = jnp.einsum("gij,is->gjs", leaf_to_child, half16(x_child), preferred_element_type=F32)
    terms = terms + jnp.einsum("gij,is->gjs", leaf_to_root, root_bf, preferred_element_type=F32)
    back_leaf = y_leaf - col_sum(terms, 8)
    x_leaf = row_sum(
        n,
        jnp.einsum("gij,gis->gjs", leaf_inv, half16(back_leaf), preferred_element_type=F32),
        9,
    )
    return (x_root, x_child[None], x_leaf, y_root)


def solution(mesh):
    in_specs = (
        P("col", None),
        P("layer", "col", None),
        P("layer", "col", None),
        P("row", "col"),
        P("layer", "row", "col"),
        P("layer", "row", "col"),
        P("layer", "col", "row"),
        P("layer", "col", "row"),
        P("layer", "col", "row"),
    )
    out_specs = (P("col", None), P("layer", "col", None), P("layer", "col", None), P("row", None))
    return jax.shard_map(
        functools.partial(on_device, mesh.shape["row"]),
        mesh=mesh,
        in_specs=in_specs,
        out_specs=out_specs,
        check_vma=False,
    )
```

time: 654 us -> 373 us (0.57)
  waiting for transfers between devices: 514 us -> 0 us
  Pallas kernels: 0 us -> 281 us
  matrix products: 116 us -> 71.2 us
  between operations: 14.2 us -> 1.27 us
    psum x10 -> x0, waiting for transfers between devices: 514 us -> none  [the longest x4 226 us: row_sum(): return lax.psum(values, 'row')]
    pallas_call x0 -> x10, Pallas kernels: none -> 281 us  [run(): pl.pallas_call(kernel, out_shape=jax.ShapeDtypeStruct((rows, values.shape...]
    dot_general x6, matrix products: 76.4 us -> 40.8 us  [the longest x1 9 us: on_device(): jnp.einsum('ij,is->js', root_half, half16(y_root), preferred_element_type...]
  transfers between devices with their start and end apart: 10 -> 0, of which waited for: 10 -> 0; matrix products, arithmetic and copies ran while one was open for 4% -> 0% of each run, Pallas kernels for 0% -> 0%
where the time goes in v1:
time: 373 us; the launch traced here: 369 us
  Pallas kernels  281 us (75%)
  matrix products  71.2 us (19%)
  local copies, waits for them, and re-layouts  14.5 us (4%)
    pallas_call x10, Pallas kernels, run(): pl.pallas_call(kernel, out_shape=jax.ShapeDtypeStruct((rows, values.shape...  281 us
    dot_general x1, matrix products, on_device(): jnp.einsum('ij,is->js', child_to_root[0], root_bf, preferred_element_type...  11.1 us
    unnamed x38, local copies, waits for them, and re-layouts  9.45 us
    dot_general x1, matrix products, on_device(): jnp.einsum('ij,is->js', root_half, half16(y_root), preferred_element_type...  9 us
    dot_general x1, matrix products, on_device(): jnp.dot(root_half, half16(r_root), preferred_element_type=F32)  8.34 us
    dot_general x1, matrix products, on_device(): jnp.dot(child_to_root[0], half16(y_child), preferred_element_type=F32)  8.32 us
    dot_general x1, matrix products, on_device(): jnp.einsum('gij,is->gjs', leaf_to_root, root_bf, preferred_element_type=F32)  8.28 us

profile of v1, /device:TPU:0, one launch (start us, length us, event | category | flops | bytes accessed | tf_op | source)
XLA Modules:
  0.0 369.3 jit_solution(15550008237381688666)
XLA Ops:
  0.6 3.9 %fusion.34 = f32[2,1024,128]{2,1,0:T(8,128)S(1)} fusion(bf16[2,1024,1024]{2,1,0:T(8,128)(2,1)} %param.14, f32[2,1024,128]{2,1,0:T(8,128)} %param.11), kind=kOutput, calls=%fused_computation.35 | convolution fusion | flops 537133056 | bytes 6291456 | tf_op jit(solution)/shard_map/gij,gjs->gis/dot_general | solution.py:312
  4.6 17.7 %shard_map.120 = f32[2048,128]{1,0:T(8,128)S(1)} custom-call(f32[2048,128]{1,0:T(8,128)S(1)} %bitcast.69), custom_call_target="tpu_custom_call" | custom-call | tf_op jit(solution)/shard_map/pallas_call | solution.py:238
  23.3 2.4 convolution_bitcast_fusion.1.d
  25.7 36.8 %shard_map.121 = f32[2048,128]{1,0:T(8,128)S(1)} custom-call(f32[2048,128]{1,0:T(8,128)S(1)} %convolution_bitcast_fusion.1.d), custom_call_target="tpu_custom_call" | custom-call | tf_op jit(solution)/shard_map/pallas_call | solution.py:238
  62.5 2.4 fusion.14.d
  64.9 16.8 %shard_map.122 = f32[2048,128]{1,0:T(8,128)S(1)} custom-call(f32[2048,128]{1,0:T(8,128)S(1)} %fusion.14.d), custom_call_target="tpu_custom_call" | custom-call | tf_op jit(solution)/shard_map/pallas_call | solution.py:238
  81.7 8.3 %fusion.2 = f32[128,4096]{0,1:T(8,128)S(1)} fusion(bf16[1,4096,2048]{2,1,0:T(8,128)(2,1)} %param.17, f32[2048,128]{1,0:T(8,128)S(1)} %shard_map.122), kind=kOutput, calls=%fused_computation.2 | convolution fusion | flops 2147745792 | bytes 19922944 | tf_op jit(solution)/shard_map/dot_general | solution.py:320
  90.1 4.5 %fusion.13.d = f32[4096,128]{1,0:T(8,128)S(1)} fusion(f32[128,4096]{0,1:T(8,128)S(1)} %fusion.2, bf16[2,4096,1024]{2,1,0:T(8,128)(2,1)S(1)} %bitcast.71, bf16[2,1024,128]{2,1,0:T(8,128)(2,1)S(1)} %bitcast.78), kind=kOutput, calls=%fused_computation.14 | convolution fusion | flops 2148007936 | bytes 21495808 | tf_op jit(solution)/shard_map/gij,gjs->is/dot_general | solution.py:315
  94.6 39.0 %shard_map.123 = f32[2048,128]{1,0:T(8,128)S(1)} custom-call(f32[4096,128]{1,0:T(8,128)S(1)} %fusion.13.d), custom_call_target="tpu_custom_call" | custom-call | tf_op jit(solution)/shard_map/pallas_call | solution.py:238
  133.7 8.3 %fusion.6.d = f32[4096,128]{1,0:T(8,128)S(1)} fusion(bf16[4096,4096]{1,0:T(8,128)(2,1)} %param.12, s32[]{:T(128)S(6)} %select_n.4, f32[2048,128]{1,0:T(8,128)S(1)} %shard_map.123, f32[4096,128]{1,0:T(8,128)S(1)} %copy-done.8), kind=kOutput, calls=%fused_computation.6 | convolution fusion | flops 2148007936 | bytes 20972544 | tf_op jit(solution)/shard_map/dot_general | solution.py:322
  142.0 30.5 %shard_map.124 = f32[4096,128]{1,0:T(8,128)S(1)} custom-call(f32[4096,128]{1,0:T(8,128)S(1)} %fusion.6.d), custom_call_target="tpu_custom_call" | custom-call | tf_op jit(solution)/shard_map/pallas_call | solution.py:238
  172.6 9.0 %fusion.4.d = f32[2048,128]{1,0:T(8,128)S(1)} fusion(bf16[4096,4096]{1,0:T(8,128)(2,1)} %param.12, s32[]{:T(128)S(6)} %select_n.4, f32[4096,128]{1,0:T(8,128)S(1)} %shard_map.124), kind=kOutput, calls=%fused_computation.4 | convolution fusion | flops 2148007936 | bytes 19922948 | tf_op jit(solution)/shard_map/ij,is->js/dot_general | solution.py:325
  181.6 39.8 %shard_map.125 = f32[4096,128]{1,0:T(8,128)S(1)} custom-call(f32[2048,128]{1,0:T(8,128)S(1)} %fusion.4.d), custom_call_target="tpu_custom_call" | custom-call | tf_op jit(solution)/shard_map/pallas_call | solution.py:238
  221.4 11.1 %fusion.20.d = f32[2048,128]{1,0:T(8,128)} fusion(bf16[1,4096,2048]{2,1,0:T(8,128)(2,1)} %param.17, f32[4096,128]{1,0:T(8,128)S(1)} %shard_map.125), kind=kOutput, calls=%fused_computation.18 | convolution fusion | flops 2148007936 | bytes 19922944 | tf_op jit(solution)/shard_map/ij,is->js/dot_general | solution.py:331
  232.5 1.2 copy-done.3
  233.7 16.7 %shard_map.126 = f32[2048,128]{1,0:T(8,128)S(1)} custom-call(f32[2048,128]{1,0:T(8,128)S(1)} %copy-done.3), custom_call_target="tpu_custom_call" | custom-call | tf_op jit(solution)/shard_map/pallas_call | solution.py:238
  250.4 6.7 %fusion.17.d = f32[2048,128]{1,0:T(8,128)S(1)} fusion(bf16[1,2048,2048]{2,1,0:T(8,128)(2,1)} %param.13, f32[2048,128]{1,0:T(8,128)S(1)} %shard_map.122, f32[2048,128]{1,0:T(8,128)S(1)} %shard_map.126), kind=kOutput, calls=%fused_computation.16 | convolution fusion | flops 1074266112 | bytes 11534336 | tf_op jit(solution)/shard_map/ij,is->js/dot_general | solution.py:335
  257.2 33.6 %shard_map.127 = f32[2048,128]{1,0:T(8,128)S(1)} custom-call(f32[2048,128]{1,0:T(8,128)S(1)} %fusion.17.d), custom_call_target="tpu_custom_call" | custom-call | tf_op jit(solution)/shard_map/pallas_call | solution.py:238
  290.8 8.3 %fusion.24 = f32[128,2,1024]{2,0,1:T(8,128)S(1)} fusion(bf16[2,4096,1024]{2,1,0:T(8,128)(2,1)} %param.16, f32[4096,128]{1,0:T(8,128)S(1)} %shard_map.125), kind=kOutput, calls=%fused_computation.22 | convolution fusion | flops 2148007936 | bytes 19922944 | tf_op jit(solution)/shard_map/gij,is->gjs/dot_general | solution.py:339
  299.1 2.3 fusion.23
  301.4 2.5 copy.17
  304.0 1.2 copy-done.4
  305.2 15.9 %shard_map.128 = f32[2048,128]{1,0:T(8,128)S(1)} custom-call(f32[2048,128]{1,0:T(8,128)S(1)} %bitcast.67), custom_call_target="tpu_custom_call" | custom-call | tf_op jit(solution)/shard_map/pallas_call | solution.py:238
  321.1 1.3 subtract_convert_fusion
  322.4 4.0 %convolution_bitcast_fusion.2 = f32[2,1024,128]{1,2,0:T(8,128)} fusion(bf16[2,1024,128]{2,1,0:T(8,128)(2,1)S(1)} %bitcast.76, bf16[2,1024,1024]{2,1,0:T(8,128)(2,1)} %param.14), kind=kOutput, calls=%fused_computation.19 | convolution fusion | flops 536870912 | bytes 5767168 | tf_op jit(solution)/shard_map/gij,gis->gjs/dot_general | solution.py:343
  326.4 2.5 copy.19
  328.9 1.4 copy-done.5
  330.3 34.1 %shard_map.129 = f32[2048,128]{1,0:T(8,128)S(1)} custom-call(f32[2048,128]{1,0:T(8,128)S(1)} %bitcast.68), custom_call_target="tpu_custom_call" | custom-call | tf_op jit(solution)/shard_map/pallas_call | solution.py:238
  364.4 1.3 copy.31
  365.7 1.0 copy.32
  366.7 1.0 copy.33
  367.7 1.3 copy.34
  (35 shorter events, 1.1 us)
Async XLA Ops:
  0.6 22.7 %copy-start.6 = (bf16[2,2048,1024]{2,1,0:T(8,128)(2,1)S(1)}, bf16[2,2048,1024]{2,1,0:T(8,128)(2,1)}, u32[]{:S(2)}) copy-start(bf16[2,2048,1024]{2,1,0:T(8,128)(2,1)} %param.15) | copy-start | bytes 25165828
  4.5 57.9 %slice-start.4 = ((s8[8388608]{0:T(1024)(128)(4,1)}), s8[4194304]{0:T(1024)(128)(4,1)S(1)}, s32[]{:S(2)}) async-start(s8[8388608]{0:T(1024)(128)(4,1)} %bitcast.72), calls=%async_computation.4 | async-start | bytes 8388608
  4.5 57.9 %copy-start.7 = (f32[1,2048,128]{2,1,0:T(8,128)S(1)}, f32[1,2048,128]{2,1,0:T(8,128)}, u32[]{:S(2)}) copy-start(f32[1,2048,128]{2,1,0:T(8,128)} %param.10) | copy-start | bytes 3145732
  22.3 1.0 copy-start
  23.3 39.2 %slice-start.5 = ((s8[8388608]{0:T(1024)(128)(4,1)}), s8[4194304]{0:T(1024)(128)(4,1)S(1)}, s32[]{:S(2)}) async-start(s8[8388608]{0:T(1024)(128)(4,1)} %bitcast.72), calls=%async_computation.5 | async-start | bytes 8388608
  62.5 27.5 %slice-start = ((s8[16777216]{0:T(1024)(128)(4,1)}), s8[4194304]{0:T(1024)(128)(4,1)S(1)}, s32[]{:S(2)}) async-start(s8[16777216]{0:T(1024)(128)(4,1)} %bitcast.70), calls=%async_computation | async-start | bytes 8388608
  62.5 27.5 %slice-start.1 = ((s8[16777216]{0:T(1024)(128)(4,1)}), s8[4194304]{0:T(1024)(128)(4,1)S(1)}, s32[]{:S(2)}) async-start(s8[16777216]{0:T(1024)(128)(4,1)} %bitcast.70), calls=%async_computation.1 | async-start | bytes 8388608
  81.7 8.4 %slice-start.2 = ((s8[16777216]{0:T(1024)(128)(4,1)}), s8[4194304]{0:T(1024)(128)(4,1)S(1)}, s32[]{:S(2)}) async-start(s8[16777216]{0:T(1024)(128)(4,1)} %bitcast.70), calls=%async_computation.2 | async-start | bytes 8388608
  81.7 8.4 %slice-start.3 = ((s8[16777216]{0:T(1024)(128)(4,1)}), s8[4194304]{0:T(1024)(128)(4,1)S(1)}, s32[]{:S(2)}) async-start(s8[16777216]{0:T(1024)(128)(4,1)} %bitcast.70), calls=%async_computation.3 | async-start | bytes 8388608
  90.1 43.6 %copy-start.8 = (f32[4096,128]{1,0:T(8,128)S(1)}, f32[4096,128]{1,0:T(8,128)}, u32[]{:S(2)}) copy-start(f32[4096,128]{1,0:T(8,128)} %param.9) | copy-start | bytes 6291460
  172.6 9.0 %copy-start.1 = (f32[4096,128]{1,0:T(8,128)}, f32[4096,128]{1,0:T(8,128)S(1)}, u32[]{:S(2)}) copy-start(f32[4096,128]{1,0:T(8,128)S(1)} %shard_map.124) | copy-start | bytes 6291460
  232.5 1.2 copy-start.3
  257.2 41.9 %slice-start.6 = ((s8[8388608]{0:T(1024)(128)(4,1)}), s8[4194304]{0:T(1024)(128)(4,1)S(1)}, s32[]{:S(2)}) async-start(s8[8388608]{0:T(1024)(128)(4,1)} %bitcast.74), calls=%async_computation.6 | async-start | bytes 8388608
  290.8 8.3 %slice-start.7 = ((s8[8388608]{0:T(1024)(128)(4,1)}), s8[4194304]{0:T(1024)(128)(4,1)S(1)}, s32[]{:S(2)}) async-start(s8[8388608]{0:T(1024)(128)(4,1)} %bitcast.74), calls=%async_computation.7 | async-start | bytes 8388608
  304.0 1.2 copy-start.4
  328.9 38.8 %copy-start.2 = (f32[4096,128]{1,0:T(8,128)S(1)}, f32[4096,128]{1,0:T(8,128)}, u32[]{:S(2)}) copy-start(f32[4096,128]{1,0:T(8,128)} %copy-done.1) | copy-start | bytes 6291460
  328.9 1.4 copy-start.5
